TPU v7x, 128 devices: a whole 4x4x4 slice. The times are simulated.
128 devices in a mesh: wide: 16 (over x_hi, y, core), narrow: 8 (over z, x_lo).
Axes of the slice: x: 4 (x_hi: 2, x_lo: 2; x = x_hi * 2 + x_lo), y: 4, z: 4, core: 2. Of those that a mesh axis runs over, the one named last changes fastest.
Arguments:
- tokens: bfloat16 [8192, 5120], P('wide', 'narrow'), may hold values from -400 to 400
- ln_gain: float32 [5120], replicated, may hold values from 0.1 to 1.9
- w_qkv: bfloat16 [5120, 10240], P('narrow', 'wide'), may hold values from -0.078125 to 0.078125
- q_gain: float32 [128], replicated, may hold values from 0.1 to 1.9
- k_gain: float32 [128], replicated, may hold values from 1 to 2
- stored_keys: bfloat16 [512, 256, 1024], P(('wide', 'narrow')), may hold values from -700 to 700
- stored_values: bfloat16 [512, 256, 1024], P(('wide', 'narrow')), may hold values from -6 to 6
- span_lengths: int32 [512], P(('wide', 'narrow')), may hold values from 1 to 16, 6144 in all
- fill_positions: int32 [512], P(('wide', 'narrow')), may hold values from 1 to 256, as said below
- w_out: bfloat16 [8192, 5120], P('wide', 'narrow'), may hold values from -0.25 to 0.25
Outputs:
- block_out: bfloat16 [8192, 5120], P('wide', 'narrow')
Inputs may be any that keep to these rules, and one draw needn't show every extreme that they name: Slots 0 to span_lengths[s] - 1 of stream s are live, the rest of its 16 slots are padding. Frames 0 to fill_positions[s] - 1 of stream s hold its past.
All inputs are finite; a program needn't handle non-finite values. No bound on the sum of `span_lengths` on one device may be relied on, other than what follows from the above.
Results may differ from a plain program's by a relative error of at most 0.006.
The roundings to bfloat16 on the way count: a program that leaves them out, or rounds other values in their place, can miss the bound.
Values may be sent and summed in bfloat16 or wider, within the bound.
No kernel may reach another device: no remote copies, remote signals or barrier semaphores. Data moves between devices by JAX's collectives and lax.ppermute only.
A program may use at most 128 MiB of HBM per device.

v0:
```python
import math

import jax
import jax.numpy as jnp
from jax import lax
from jax.sharding import PartitionSpec as P

D = 5120
QUERY_HEADS = 64
KEY_VALUE_HEADS = 8
HEAD_SIZE = 128


EPSILON = 1e-06
ROPE_BASE = 1000000.0


def head_norm(vectors, gains):
    mean_square = jnp.mean(vectors * vectors, axis=-1, keepdims=True)
    return vectors * lax.rsqrt(mean_square + EPSILON) * gains


def rotate(vectors, position):
    half_dim = vectors.shape[-1] // 2
    frequency = jnp.exp(
        jnp.arange(half_dim, dtype=jnp.float32) * (-2.0 * math.log(ROPE_BASE) / vectors.shape[-1])
    )
    angles = position[:, None] * frequency[None, :]
    cosine = jnp.cos(angles)[:, None, :]
    sine_part = jnp.sin(angles)[:, None, :]
    first_half = vectors[..., :half_dim]
    second_half = vectors[..., half_dim:]
    return jnp.concatenate(
        [
            first_half * cosine - second_half * sine_part,
            second_half * cosine + first_half * sine_part,
        ],
        axis=-1,
    )


def attend(
    packed,
    own_squares,
    head_groups,
    q_gain,
    k_gain,
    stored_keys,
    stored_values,
    span_lengths,
    fill_positions,
):
    stream_list = span_lengths.shape[0]
    total_row_count = packed.shape[0]
    cache_slot_count = total_row_count // stream_list
    cache_frame_count = stored_keys.shape[1]
    query_group_size = QUERY_HEADS // KEY_VALUE_HEADS
    query_columns = QUERY_HEADS * HEAD_SIZE // head_groups
    key_columns = KEY_VALUE_HEADS * HEAD_SIZE // head_groups
    grouped_queries = packed.reshape(total_row_count, head_groups, query_columns + 2 * key_columns)
    query_raw = (
        grouped_queries[:, :, :query_columns]
        .reshape(total_row_count, QUERY_HEADS, HEAD_SIZE)
        .astype(jnp.float32)
    )
    unnormed_key = (
        grouped_queries[:, :, query_columns : query_columns + key_columns]
        .reshape(total_row_count, KEY_VALUE_HEADS, HEAD_SIZE)
        .astype(jnp.float32)
    )
    unnormed_value = (
        grouped_queries[:, :, query_columns + key_columns :]
        .reshape(total_row_count, KEY_VALUE_HEADS * HEAD_SIZE)
        .astype(jnp.float32)
    )
    inverse_root_mean = lax.rsqrt(own_squares / D + EPSILON)
    fresh_values = (
        (unnormed_value * inverse_root_mean[:, None])
        .astype(jnp.bfloat16)
        .reshape(stream_list, cache_slot_count, KEY_VALUE_HEADS, HEAD_SIZE)
    )
    slot_index = jnp.arange(cache_slot_count, dtype=jnp.int32)
    position = (
        (fill_positions[:, None] + slot_index[None, :]).reshape(total_row_count).astype(jnp.float32)
    )
    query_rows = rotate(head_norm(query_raw, q_gain), position).astype(jnp.bfloat16)
    query_rows = query_rows.reshape(
        stream_list, cache_slot_count, KEY_VALUE_HEADS, query_group_size, HEAD_SIZE
    )
    fresh_keys = rotate(head_norm(unnormed_key, k_gain), position).astype(jnp.bfloat16)
    fresh_keys = fresh_keys.reshape(stream_list, cache_slot_count, KEY_VALUE_HEADS, HEAD_SIZE)
    earlier_keys = stored_keys.reshape(stream_list, cache_frame_count, KEY_VALUE_HEADS, HEAD_SIZE)
    earlier_values = stored_values.reshape(
        stream_list, cache_frame_count, KEY_VALUE_HEADS, HEAD_SIZE
    )
    score_scale = 1.0 / math.sqrt(HEAD_SIZE)
    old_scores = (
        jnp.einsum(
            "sckgd,sfkd->skgcf", query_rows, earlier_keys, preferred_element_type=jnp.float32
        )
        * score_scale
    )
    new_scores = (
        jnp.einsum("sckgd,sjkd->skgcj", query_rows, fresh_keys, preferred_element_type=jnp.float32)
        * score_scale
    )
    frame_index = jnp.arange(cache_frame_count, dtype=jnp.int32)
    old_live = (frame_index[None, :] < fill_positions[:, None])[:, None, None, None, :]
    new_live = (slot_index[None, None, :] <= slot_index[None, :, None]) & (
        slot_index[None, None, :] < span_lengths[:, None, None]
    )
    new_live = new_live[:, None, None, :, :]
    old_scores = jnp.where(old_live, old_scores, -1e30)
    new_scores = jnp.where(new_live, new_scores, -1e30)
    row_max = jnp.maximum(
        jnp.max(old_scores, axis=-1, keepdims=True), jnp.max(new_scores, axis=-1, keepdims=True)
    )
    old_weights = jnp.exp(old_scores - row_max)
    new_weights = jnp.exp(new_scores - row_max)
    denominator = jnp.sum(old_weights, axis=-1) + jnp.sum(new_weights, axis=-1)
    mixed_heads = jnp.einsum(
        "skgcf,sfkd->sckgd",
        old_weights.astype(jnp.bfloat16),
        earlier_values,
        preferred_element_type=jnp.float32,
    )
    mixed_heads = mixed_heads + jnp.einsum(
        "skgcj,sjkd->sckgd",
        new_weights.astype(jnp.bfloat16),
        fresh_values,
        preferred_element_type=jnp.float32,
    )
    mixed_heads = mixed_heads / jnp.transpose(denominator, (0, 3, 1, 2))[..., None]
    query_live = (slot_index[None, :] < span_lengths[:, None])[:, :, None, None, None]
    mixed_heads = jnp.where(query_live, mixed_heads, 0.0)
    return mixed_heads.reshape(total_row_count, QUERY_HEADS * HEAD_SIZE).astype(jnp.bfloat16)


def shards(
    tokens,
    ln_gain,
    w_qkv,
    q_gain,
    k_gain,
    stored_keys,
    stored_values,
    span_lengths,
    fill_positions,
    w_out,
):
    wide_count = lax.axis_size("wide")
    narrow_count = lax.axis_size("narrow")
    total_row_count = tokens.shape[0] // narrow_count
    feature_part = tokens.shape[1]
    local_tokens = tokens.reshape(narrow_count, total_row_count, feature_part)
    gathered = lax.all_gather(local_tokens, "wide", axis=1, tiled=True)
    flattened = gathered.reshape(narrow_count * wide_count * total_row_count, feature_part)
    gain_part = lax.dynamic_slice_in_dim(
        ln_gain, lax.axis_index("narrow") * feature_part, feature_part
    )
    token_values = flattened.astype(jnp.float32)
    normed = (token_values * gain_part[None, :]).astype(jnp.bfloat16)
    partial_terms = jnp.dot(normed, w_qkv, preferred_element_type=jnp.float32)
    squares = jnp.sum(token_values * token_values, axis=1)
    summed, square_sums = (
        lax.psum_scatter(partial_terms, "narrow", scatter_dimension=0, tiled=True),
        lax.psum_scatter(squares, "narrow", scatter_dimension=0, tiled=True),
    )
    own_squares = lax.dynamic_slice_in_dim(
        square_sums, lax.axis_index("wide") * total_row_count, total_row_count
    )
    packed = lax.all_to_all(
        summed.astype(jnp.bfloat16), "wide", split_axis=0, concat_axis=1, tiled=True
    )
    attended = attend(
        packed,
        own_squares,
        wide_count,
        q_gain,
        k_gain,
        stored_keys,
        stored_values,
        span_lengths,
        fill_positions,
    )
    every_row = lax.all_gather(attended, "narrow", axis=0, tiled=True)
    result = jnp.dot(
        every_row,
        lax.all_gather(w_out, "wide", axis=0, tiled=True),
        preferred_element_type=jnp.float32,
    )
    return result.astype(jnp.bfloat16)


def solution(mesh):
    placed = (
        P("wide", "narrow"),
        P(),
        P("narrow", "wide"),
        P(),
        P(),
        P(("wide", "narrow"), None, None),
        P(("wide", "narrow"), None, None),
        P(("wide", "narrow")),
        P(("wide", "narrow")),
        P("wide", "narrow"),
    )
    return jax.shard_map(
        shards, mesh=mesh, in_specs=placed, out_specs=P("wide", "narrow"), check_vma=False
    )
```

profile of v0, /device:TPU:0, one launch (start us, length us, event | category | flops | bytes accessed | tf_op | source)
XLA Modules:
  0.0 806.0 jit_solution(16724693437596249020)
XLA Ops:
  6.5 0.7 all-gather.4.cloned.1.call-update
  7.3 0.0 reduce-scatter.2.cloned.1.call-start
  7.3 0.8 dynamic_slice.6
  8.1 86.1 %all-gather.4.cloned.1.call-done = bf16[8,1024,640]{2,1,0:T(8,128)(2,1)} async-done(((bf16[8,64,640]{2,1,0:T(8,128)(2,1)}), bf16[8,1024,640]{2,1,0:T(8,128)(2,1)}) %all-gather.4.cloned.1.call-update) | async-done | bytes 10485776 | tf_op jit(solution)/shard_map/all_gather | solution.py:156
  94.2 10.0 %fusion = bf16[8192,640]{1,0:T(8,128)(2,1)} fusion(f32[640]{0:T(1024)S(1)} %dynamic_slice.6, bf16[8,1024,640]{2,1,0:T(8,128)(2,1)} %all-gather.4.cloned.1.call-done), kind=kLoop, calls=%fused_computation.1 | loop fusion | flops 15728640 | bytes 20974080 | tf_op jit(solution)/shard_map/convert_element_type | solution.py:162
  104.2 15.9 %fusion.24 = f32[8192,640]{1,0:T(8,128)} fusion(bf16[8192,640]{1,0:T(8,128)(2,1)} %fusion, bf16[640,640]{1,0:T(8,128)(2,1)S(1)} %copy-done), kind=kOutput, calls=%fused_computation.61 | convolution fusion | flops 6710886400 | bytes 32276480 | tf_op jit(solution)/shard_map/dot_general | solution.py:163
  120.1 0.0 reduce-scatter.2.cloned.1.call-update
  120.1 0.0 all-gather.8.cloned.1.call-start
  120.2 0.7 all-gather.8.cloned.1.call-update
  120.9 0.1 add_convert_fusion.2
  120.9 0.1 convert_element_type.77
  121.0 0.7 copy-done.5
  121.7 2.0 copy.105
  123.7 0.6 copy.106
  124.3 0.6 dynamic-slice
  125.6 0.1 iota_compare_fusion.2
  125.7 0.1 iota_compare_fusion.1
  125.7 0.1 broadcast_and_fusion
  125.8 0.2 multiply_cosine_fusion
  126.0 3.7 bitcast_bitcast_fusion.1
  129.7 393.6 %reduce-scatter.2.cloned.1.call-done = f32[1024,640]{1,0:T(8,128)} async-done(((f32[8192,640]{1,0:T(8,128)}), f32[1024,640]{1,0:T(8,128)}) %reduce-scatter.2.cloned.1.call-update) | async-done | bytes 2621456 | tf_op jit(solution)/shard_map/reduce_scatter | solution.py:166
  523.3 2.9 convert_element_type.73
  526.3 6.6 all-to-all-start
  532.8 0.0 all-gather.6.cloned.1.call-start
  532.9 1.5 bitcast_bitcast_fusion
  534.4 6.7 multiply_reduce_fusion
  541.1 42.6 %all-reduce = f32[8192]{0:T(1024)S(1)} all-reduce(f32[8192]{0:T(1024)S(1)} %bitcast.82), channel_id=3, replica_groups=mesh['wide'=16,'narrow'=8] {'narrow'}, use_global_device_ids=true, to_apply=%region_7.8.clone | all-reduce | flops 8192 | bytes 65536
  583.7 0.1 add_rsqrt_fusion.2
  583.8 0.1 mul.211
  583.9 1.5 slice_convert_fusion
  585.4 2.5 copy.70
  587.9 1.6 reshape.220
  589.6 1.2 slice_convert_fusion.1
  590.8 0.3 copy.74
  591.1 0.8 reshape.221
  591.9 1.2 multiply_reduce_fusion.2
  593.1 0.1 copy.77
  593.2 1.1 multiply_multiply_fusion.1
  594.3 0.2 subtract_convert_fusion.1
  594.5 0.6 multiply_reduce_fusion.1
  595.2 0.7 multiply_multiply_fusion
  595.9 0.9 subtract_convert_fusion
  596.8 0.6 pad_maximum_fusion
  597.4 1.0 copy-done.4
  598.4 2.9 bitcast_reduce_fusion
  601.3 0.1 copy.81
  601.4 4.0 fusion.23
  605.4 0.1 copy.82
  605.5 2.3 fusion.12
  607.8 0.1 copy.88
  607.9 3.9 fusion.2
  611.9 0.8 copy.89
  612.7 0.3 copy.85
  613.0 0.1 reshape.222
  613.1 0.1 fusion.18
  613.3 0.3 copy-done.2
  613.5 2.5 fusion.7
  616.1 1.2 fusion.6
  617.3 0.3 copy.90
  617.6 1.5 convert_element_type.88
  619.1 0.0 all-gather.6.cloned.1.call-update
  619.1 0.0 all-gather.8.cloned.1.call-done
  619.1 167.4 %all-gather.6.cloned.1.call-done = bf16[512,8192]{1,0:T(8,128)(2,1)} async-done(((bf16[64,8192]{1,0:T(8,128)(2,1)}), bf16[512,8192]{1,0:T(8,128)(2,1)}) %all-gather.6.cloned.1.call-update) | async-done | bytes 8388624 | tf_op jit(solution)/shard_map/all_gather | solution.py:186
  786.5 12.9 %convolution_convert_fusion = bf16[512,640]{1,0:T(8,128)(2,1)} fusion(bf16[512,8192]{1,0:T(8,128)(2,1)} %all-gather.6.cloned.1.call-done, bf16[8192,640]{1,0:T(8,128)(2,1)} %all-gather.8.cloned.1.call-done), kind=kOutput, calls=%fused_computation.28 | convolution fusion | flops 5369036800 | bytes 19529728 | tf_op jit(solution)/shard_map/dot_general | solution.py:187
  (35 shorter events, 0.2 us)
Async XLA Ops:
  6.5 97.6 %copy-start = (bf16[640,640]{1,0:T(8,128)(2,1)S(1)}, bf16[640,640]{1,0:T(8,128)(2,1)}, u32[]{:S(2)}) copy-start(bf16[640,640]{1,0:T(8,128)(2,1)} %param.12) | copy-start | bytes 2457604
  6.5 87.6 %all-gather.4.cloned.1.call-start = ((), (), s32[]{:S(2)}) async-start(), calls=%async_computation.2 | async-start | bytes 11141120 | tf_op jit(solution)/shard_map/all_gather | solution.py:156
  7.3 516.1 %reduce-scatter.2.cloned.1.call-start = ((), (), s32[]{:S(2)}) async-start(), calls=%async_computation.3 | async-start | bytes 23592960 | tf_op jit(solution)/shard_map/reduce_scatter | solution.py:166
  120.1 0.8 copy-start.10
  120.1 1.6 copy-start.5
  120.1 499.0 %all-gather.8.cloned.1.call-start = ((), (), s32[]{:S(2)}) async-start(), calls=%async_computation.5 | async-start | bytes 11141120 | tf_op jit(solution)/shard_map/all_gather | solution.py:189
  121.7 2.0 copy-start.6
  123.7 0.7 copy-start.12
  123.7 1.9 copy-start.11
  526.3 57.6 %all-to-all-start = ((bf16[16,64,640]{2,1,0:T(8,128)(2,1)}), bf16[16,64,640]{2,1,0:T(8,128)(2,1)}, u32[]{:S(2)}, u32[]{:S(2)}) async-start(bf16[16,64,640]{2,1,0:T(8,128)(2,1)} %bitcast.73), calls=%async_computation.1 | async-start | bytes 2621440 | tf_op jit(solution)/shard_map/all_to_all | solution.py:172
  532.8 253.7 %all-gather.6.cloned.1.call-start = ((), (), s32[]{:S(2)}) async-start(), calls=%async_computation.4 | async-start | bytes 9437184 | tf_op jit(solution)/shard_map/all_gather | solution.py:186
  589.6 3.7 copy-start.8
  593.1 2.1 copy-start.9
  596.8 1.6 copy-start.4
  611.9 1.7 copy-start.2
  613.5 2.5 copy-start.3
  613.5 2.5 copy-start.7
  786.5 12.9 %copy-start.1 = (bf16[640,640]{1,0:T(8,128)(2,1)S(1)}, bf16[640,640]{1,0:T(8,128)(2,1)}, u32[]{:S(2)}) copy-start(bf16[640,640]{1,0:T(8,128)(2,1)} %param.12) | copy-start | bytes 2457604
Sparse Core Ops, SparseCore 0:
  9.9 84.2 all-gather.3
  120.2 403.0 reduce-scatter.1
  525.8 91.3 all-gather.7
  619.2 167.2 all-gather.5
where the time goes:
time: 807 us; the launch traced here: 806 us
  waiting for transfers between devices  649 us (80%)
  blocking collectives  42.6 us (5%)
  matrix products  39.3 us (5%)
  other arithmetic  34.6 us (4%)
  local copies, waits for them, and re-layouts  20.1 us (2%)
  between operations  14.1 us (2%)
    reduce_scatter x1, waiting for transfers between devices, shards(): lax.psum_scatter(partial_terms, 'narrow', scatter_dimension=0, tiled=True)  394 us
    all_gather x1, waiting for transfers between devices, shards(): every_row = lax.all_gather(attended, 'narrow', axis=0, tiled=True)  167 us
    all_gather x1, waiting for transfers between devices, shards(): gathered = lax.all_gather(local_tokens, 'wide', axis=1, tiled=True)  86.1 us
    unnamed x1, blocking collectives  42.6 us
  transfers between devices with their start and end apart: 5, of which 3 were waited for; matrix products, arithmetic and copies ran while one was open for 7% of the time, Pallas kernels for 0%

commit v1 on v0

--- a/solution.py
+++ b/solution.py
@@ -149,28 +149,15 @@
     w_out,
 ):
     wide_count = lax.axis_size("wide")
-    narrow_count = lax.axis_size("narrow")
-    total_row_count = tokens.shape[0] // narrow_count
-    feature_part = tokens.shape[1]
-    local_tokens = tokens.reshape(narrow_count, total_row_count, feature_part)
-    gathered = lax.all_gather(local_tokens, "wide", axis=1, tiled=True)
-    flattened = gathered.reshape(narrow_count * wide_count * total_row_count, feature_part)
-    gain_part = lax.dynamic_slice_in_dim(
-        ln_gain, lax.axis_index("narrow") * feature_part, feature_part
-    )
-    token_values = flattened.astype(jnp.float32)
-    normed = (token_values * gain_part[None, :]).astype(jnp.bfloat16)
-    partial_terms = jnp.dot(normed, w_qkv, preferred_element_type=jnp.float32)
-    squares = jnp.sum(token_values * token_values, axis=1)
-    summed, square_sums = (
-        lax.psum_scatter(partial_terms, "narrow", scatter_dimension=0, tiled=True),
-        lax.psum_scatter(squares, "narrow", scatter_dimension=0, tiled=True),
-    )
-    own_squares = lax.dynamic_slice_in_dim(
-        square_sums, lax.axis_index("wide") * total_row_count, total_row_count
-    )
+    own_rows = lax.all_to_all(tokens, "narrow", split_axis=0, concat_axis=1, tiled=True)
+    token_values = own_rows.astype(jnp.float32)
+    own_squares = jnp.sum(token_values * token_values, axis=1)
+    normed = (token_values * ln_gain[None, :]).astype(jnp.bfloat16)
+    every_normed = lax.all_gather(normed, "wide", axis=0, tiled=True)
+    columns = lax.all_gather(w_qkv, "narrow", axis=0, tiled=True)
+    projected = jnp.dot(every_normed, columns, preferred_element_type=jnp.float32)
     packed = lax.all_to_all(
-        summed.astype(jnp.bfloat16), "wide", split_axis=0, concat_axis=1, tiled=True
+        projected.astype(jnp.bfloat16), "wide", split_axis=0, concat_axis=1, tiled=True
     )
     attended = attend(
         packed,

time: 807 us -> 513 us (0.64)
  waiting for transfers between devices: 649 us -> 406 us
  blocking collectives: 42.6 us -> 19.4 us
  other arithmetic: 34.6 us -> 12.1 us
    reduce_scatter x1 -> x0, waiting for transfers between devices: 394 us -> none  [shards(): lax.psum_scatter(partial_terms, 'narrow', scatter_dimension=0, tiled=True)]
    all_gather x1 -> x2, waiting for transfers between devices: 86.1 us -> 199 us  [the longest x1 113 us: shards(): columns = lax.all_gather(w_qkv, 'narrow', axis=0, tiled=True)]
    unnamed x1 -> x0, blocking collectives: 42.6 us -> none
    all_gather x1, waiting for transfers between devices: 0.02 us -> 19.4 us  [shards(): lax.all_gather(w_out, 'wide', axis=0, tiled=True)]
    all_to_all x0 -> x1, blocking collectives: none -> 19.4 us  [shards(): lax.all_to_all(tokens, 'narrow', split_axis=0, concat_axis=1, tiled=True)]
    all_to_all x1, waiting for transfers between devices: 0.01 us -> 19.1 us  [shards(): lax.all_to_all(projected.astype(jnp.bfloat16), 'wide', split_axis=0, conc...]
    convert_element_type x2 -> x1, other arithmetic: 12.9 us -> 0.92 us  [shards(): normed = (token_values * ln_gain[None, :]).astype(jnp.bfloat16)]
  transfers between devices with their start and end apart: 5 -> 5, of which waited for: 3 -> 5; matrix products, arithmetic and copies ran while one was open for 7% -> 10% of each run, Pallas kernels for 0% -> 0%
where the time goes in v1:
time: 513 us; the launch traced here: 512 us
  waiting for transfers between devices  406 us (79%)
  matrix products  35.8 us (7%)
  local copies, waits for them, and re-layouts  21 us (4%)
  blocking collectives  19.4 us (4%)
  between operations  13.5 us (3%)
  other arithmetic  12.1 us (2%)
    all_gather x1, waiting for transfers between devices, shards(): every_row = lax.all_gather(attended, 'narrow', axis=0, tiled=True)  168 us
    all_gather x1, waiting for transfers between devices, shards(): columns = lax.all_gather(w_qkv, 'narrow', axis=0, tiled=True)  113 us
    all_gather x1, waiting for transfers between devices, shards(): every_normed = lax.all_gather(normed, 'wide', axis=0, tiled=True)  85.3 us
    all_gather x1, waiting for transfers between devices, shards(): lax.all_gather(w_out, 'wide', axis=0, tiled=True)  19.4 us
    all_to_all x1, blocking collectives, shards(): lax.all_to_all(tokens, 'narrow', split_axis=0, concat_axis=1, tiled=True)  19.4 us
    all_to_all x1, waiting for transfers between devices, shards(): lax.all_to_all(projected.astype(jnp.bfloat16), 'wide', split_axis=0, conc...  19.1 us
    dot_general x1, matrix products, shards(): jnp.dot(every_normed, columns, preferred_element_type=jnp.float32)  13.7 us
    dot_general x1, matrix products, shards(): jnp.dot(every_row, lax.all_gather(w_out, 'wide', axis=0, tiled=True), pre...  12.8 us
  transfers between devices with their start and end apart: 5, of which 5 were waited for; matrix products, arithmetic and copies ran while one was open for 10% of the time, Pallas kernels for 0%

profile of v1, /device:TPU:0, one launch (start us, length us, event | category | flops | bytes accessed | tf_op | source)
XLA Modules:
  0.0 511.8 jit_solution(5610698317668824876)
XLA Ops:
  6.5 0.7 all-gather.7.cloned.1.call-update
  7.3 0.0 all-gather.5.cloned.1.call-start
  7.3 19.4 %all_to_all.29 = bf16[8,64,640]{2,1,0:T(8,128)(2,1)S(1)} all-to-all(bf16[8,64,640]{2,1,0:T(8,128)(2,1)} %bitcast.77), channel_id=1, replica_groups=mesh['wide'=16,'narrow'=8] {'narrow'}, dimensions={0} | all-to-all | bytes 1310720 | tf_op jit(solution)/shard_map/all_to_all | solution.py:152
  26.7 0.8 copy-done.4
  27.5 0.1 convert_bitcast_fusion
  27.6 0.1 copy.109
  27.7 0.5 copy-done.9
  28.3 0.9 multiply_convert_fusion
  29.2 0.0 all-gather.5.cloned.1.call-update
  29.2 0.0 all-gather.11.cloned.1.call-start
  29.2 0.7 all-gather.11.cloned.1.call-update
  29.9 0.1 add_convert_fusion.2
  30.0 0.1 convert_element_type.82
  30.1 2.0 copy.110
  32.1 0.6 copy.111
  32.7 0.1 iota_compare_fusion.2
  32.8 0.1 broadcast_and_fusion
  32.9 0.2 multiply_cosine_fusion
  33.1 113.4 %all-gather.7.cloned.1.call-done = bf16[5120,640]{1,0:T(8,128)(2,1)} async-done(((bf16[640,640]{1,0:T(8,128)(2,1)}), bf16[5120,640]{1,0:T(8,128)(2,1)}) %all-gather.7.cloned.1.call-update) | async-done | bytes 6553616 | tf_op jit(solution)/shard_map/all_gather | solution.py:157
  146.5 85.3 %all-gather.5.cloned.1.call-done = bf16[1024,5120]{1,0:T(8,128)(2,1)} async-done(((bf16[64,5120]{1,0:T(8,128)(2,1)}), bf16[1024,5120]{1,0:T(8,128)(2,1)}) %all-gather.5.cloned.1.call-update) | async-done | bytes 10485776 | tf_op jit(solution)/shard_map/all_gather | solution.py:156
  231.7 13.7 %convolution_convert_fusion = bf16[1024,640]{1,0:T(8,128)(2,1)} fusion(bf16[1024,5120]{1,0:T(8,128)(2,1)} %all-gather.5.cloned.1.call-done, bf16[5120,640]{1,0:T(8,128)(2,1)} %all-gather.7.cloned.1.call-done), kind=kOutput, calls=%fused_computation.27 | convolution fusion | flops 6711541760 | bytes 18350080 | tf_op jit(solution)/shard_map/dot_general | solution.py:158
  245.5 3.7 all-to-all-start.1
  249.2 0.0 all-gather.9.cloned.1.call-start
  249.2 0.1 iota_compare_fusion.1
  249.3 3.1 bitcast_bitcast_fusion.1
  252.4 1.4 bitcast_bitcast_fusion
  253.8 0.2 fusion.13
  254.1 0.1 rsqrt.29
  254.1 19.1 %all-to-all-done.1 = bf16[16,64,640]{2,1,0:T(8,128)(2,1)S(1)} async-done(((bf16[16,64,640]{2,1,0:T(8,128)(2,1)}), bf16[16,64,640]{2,1,0:T(8,128)(2,1)S(1)}, u32[]{:S(2)}, u32[]{:S(2)}) %all-to-all-start.1) | async-done | bytes 1310752 | tf_op jit(solution)/shard_map/all_to_all | solution.py:159
  273.3 0.3 slice_convert_fusion
  273.5 2.6 copy.74
  276.1 1.6 reshape.227
  277.7 0.9 slice_convert_fusion.1
  278.7 1.1 copy.78
  279.8 2.0 reshape.228
  281.9 0.2 multiply_reduce_fusion.1
  282.1 0.1 copy.81
  282.2 1.1 multiply_multiply_fusion.1
  283.3 0.2 subtract_convert_fusion.1
  283.5 0.6 multiply_reduce_fusion
  284.2 0.7 multiply_multiply_fusion
  284.9 0.9 subtract_convert_fusion
  285.8 0.6 pad_maximum_fusion
  286.4 1.1 copy-done.3
  287.5 3.0 bitcast_reduce_fusion
  290.4 0.1 copy.85
  290.5 2.6 fusion.23
  293.2 0.1 copy.86
  293.3 0.7 fusion.11
  294.0 0.1 copy.92
  294.1 0.4 copy-done.1
  294.5 4.0 fusion.1
  298.5 0.1 copy.93
  298.6 0.3 copy.89
  298.9 0.1 reshape.229
  299.1 0.1 fusion.18
  299.2 0.9 copy-done
  300.1 2.5 fusion.6
  302.6 1.2 fusion.5
  303.8 0.3 copy.94
  304.1 1.3 convert_element_type.93
  305.4 19.4 %all-gather.11.cloned.1.call-done = bf16[8192,640]{1,0:T(8,128)(2,1)} async-done(((bf16[512,640]{1,0:T(8,128)(2,1)}), bf16[8192,640]{1,0:T(8,128)(2,1)}) %all-gather.11.cloned.1.call-update) | async-done | bytes 10485776 | tf_op jit(solution)/shard_map/all_gather | solution.py:176
  324.8 167.6 %all-gather.9.cloned.1.call-done = bf16[512,8192]{1,0:T(8,128)(2,1)} async-done(((bf16[64,8192]{1,0:T(8,128)(2,1)}), bf16[512,8192]{1,0:T(8,128)(2,1)}) %all-gather.9.cloned.1.call-update) | async-done | bytes 8388624 | tf_op jit(solution)/shard_map/all_gather | solution.py:173
  492.4 12.8 %convolution_convert_fusion.1 = bf16[512,640]{1,0:T(8,128)(2,1)} fusion(bf16[512,8192]{1,0:T(8,128)(2,1)} %all-gather.9.cloned.1.call-done, bf16[8192,640]{1,0:T(8,128)(2,1)} %all-gather.11.cloned.1.call-done), kind=kOutput, calls=%fused_computation.28 | convolution fusion | flops 5369036800 | bytes 19529728 | tf_op jit(solution)/shard_map/dot_general | solution.py:174
  (39 shorter events, 0.2 us)
Async XLA Ops:
  6.5 140.0 %all-gather.7.cloned.1.call-start = ((), (), s32[]{:S(2)}) async-start(), calls=%async_computation.3 | async-start | bytes 7372800 | tf_op jit(solution)/shard_map/all_gather | solution.py:157
  7.3 224.5 %all-gather.5.cloned.1.call-start = ((), (), s32[]{:S(2)}) async-start(), calls=%async_computation.2 | async-start | bytes 11141120 | tf_op jit(solution)/shard_map/all_gather | solution.py:156
  26.7 0.8 copy-start.4
  27.5 0.7 copy-start.9
  27.7 2.2 copy-start.12
  27.7 2.4 copy-start.7
  29.2 295.6 %all-gather.11.cloned.1.call-start = ((), (), s32[]{:S(2)}) async-start(), calls=%async_computation.5 | async-start | bytes 11141120 | tf_op jit(solution)/shard_map/all_gather | solution.py:176
  30.1 2.0 copy-start.8
  32.1 0.7 copy-start.15
  32.8 212.7 %copy-start.13 = (pred[4,16]{1,0:T(4,128)(4,1)}, pred[4,16]{1,0:T(4,128)(4,1)S(1)}, u32[]{:S(2)}) copy-start(pred[4,16]{1,0:T(4,128)(4,1)S(1)} %iota_compare_fusion.2) | copy-start | bytes 196
  245.5 27.8 %all-to-all-start.1 = ((bf16[16,64,640]{2,1,0:T(8,128)(2,1)}), bf16[16,64,640]{2,1,0:T(8,128)(2,1)S(1)}, u32[]{:S(2)}, u32[]{:S(2)}) async-start(bf16[16,64,640]{2,1,0:T(8,128)(2,1)} %bitcast.76), calls=%async_computation.1 | async-start | bytes 2621440 | tf_op jit(solution)/shard_map/all_to_all | solution.py:159
  249.2 243.2 %all-gather.9.cloned.1.call-start = ((), (), s32[]{:S(2)}) async-start(), calls=%async_computation.4 | async-start | bytes 9437184 | tf_op jit(solution)/shard_map/all_gather | solution.py:173
  252.4 1.4 copy-start.5
  277.7 4.5 copy-start.10
  282.1 2.1 copy-start.11
  285.8 1.7 copy-start.3
  293.2 1.3 copy-start.1
  294.5 4.1 copy-start.6
  298.5 1.6 copy-start
  300.1 2.5 copy-start.2
  300.1 2.5 copy-start.14
Sparse Core Ops, SparseCore 0:
  9.0 137.4 all-gather.6
  149.0 82.7 all-gather.4
  234.2 90.5 all-gather.10
  326.3 166.0 all-gather.8
